TPU v7x, 32 devices: a whole 2x2x4 slice. The times are simulated.
32 devices in a mesh: seq: 8 (over z, y), mp: 4 (over x, core).
Axes of the slice: x: 2, y: 2, z: 4, core: 2. Of those that a mesh axis runs over, the one named last changes fastest.
Arguments:
- q_branch: bfloat16 [16, 128, 2048], P('seq', None, 'mp'), may hold values from -4.5 to 4.5
- k_branch: bfloat16 [16, 128, 2048], P('seq', None, 'mp'), may hold values from -6 to 6
- v_branch: bfloat16 [16, 128, 2048], P('seq', None, 'mp'), may hold values from -6 to 6
- d_out: bfloat16 [16, 128, 2048], P('seq', 'mp'), may hold values from -24 to 24
- k_prefix: bfloat16 [768, 1, 2048], P('seq', None, 'mp'), may hold values from -4.5 to 4.5
- v_prefix: bfloat16 [768, 1, 2048], P('seq', None, 'mp'), may hold values from -6 to 6
- slot_branch: int32 [16], replicated, may hold values from 0 to 15, each once
- branch_len: int32 [16], replicated, may hold values from 1 to 128, 1280 in all
Outputs:
- query_grad: bfloat16 [16, 128, 2048], P('seq', None, 'mp')
- branch_key_grad: bfloat16 [16, 128, 2048], P('seq', None, 'mp')
- branch_value_grad: bfloat16 [16, 128, 2048], P('seq', None, 'mp')
- prefix_key_grad: bfloat16 [768, 1, 2048], P('seq', None, 'mp')
- prefix_value_grad: bfloat16 [768, 1, 2048], P('seq', None, 'mp')
Inputs may be any that keep to these rules, and one draw needn't show every extreme that they name: `slot_branch`: each branch stands in exactly one slot. `branch_len`: some branch has exactly 128 frames.
All inputs are finite; a program needn't handle non-finite values.
Results may differ from a plain program's by a relative error of at most 0.0084.
Values may be sent and summed in bfloat16 or wider, within the bound.
A program may use at most 128 MiB of HBM per device.

v0:
```python
import math

import jax
import jax.numpy as jnp
from jax import lax
from jax.sharding import PartitionSpec as P

HEAD = 128


def pick_prefix(gathered, slot_count):
    row_list = [gathered[:, 0] for slot_index in range(slot_count)]
    return jnp.stack(row_list, 0)


def by_prefix(grad_rows):
    summed = grad_rows[0]
    summed = summed + grad_rows[1]
    return summed[:, None, :]


def merge_heads(stacked):
    head_count, slot_count, frames, width = stacked.shape
    return jnp.transpose(stacked, (1, 2, 0, 3)).reshape(slot_count, frames, head_count * width)


def merge_prefix(stacked):
    head_count, prefix_rows, prefix_count, width = stacked.shape
    return jnp.transpose(stacked, (1, 2, 0, 3)).reshape(
        prefix_rows, prefix_count, head_count * width
    )


def body(q_branch, k_branch, v_branch, d_out, k_prefix, v_prefix, slot_branch, branch_len):
    score_scale = 1.0 / math.sqrt(HEAD)
    slot_count = q_branch.shape[0]
    frames = q_branch.shape[1]
    local_heads = q_branch.shape[2] // HEAD
    own_branches = lax.dynamic_slice_in_dim(
        slot_branch, lax.axis_index("seq") * slot_count, slot_count
    )
    branch_hits = (
        own_branches[:, None] == jnp.arange(slot_branch.shape[0], dtype=jnp.int32)[None, :]
    )
    lengths = jnp.sum(jnp.where(branch_hits, branch_len[None, :], 0), 1)
    cotangent = lax.all_to_all(d_out, "mp", split_axis=2, concat_axis=1, tiled=True)
    live_rows = jnp.arange(frames, dtype=jnp.int32)[None, :, None] < lengths[:, None, None]
    masked = jnp.where(live_rows, cotangent, jnp.zeros_like(cotangent))
    prefix_keys, prefix_values = (
        lax.all_gather(k_prefix, "seq", axis=0, tiled=True),
        lax.all_gather(v_prefix, "seq", axis=0, tiled=True),
    )
    prefix_rows = prefix_keys.shape[0]
    key_pick = pick_prefix(prefix_keys, slot_count)
    value_pick = pick_prefix(prefix_values, slot_count)
    query_pos = jnp.arange(frames, dtype=jnp.int32)[:, None]
    key_pos = jnp.arange(prefix_rows + frames, dtype=jnp.int32)[None, :] - prefix_rows
    allowed = (key_pos <= query_pos)[None]

    def per_head(head_index):
        column_start = head_index * HEAD
        query_head = lax.dynamic_slice_in_dim(q_branch, column_start, HEAD, 2)
        cotangent_head = lax.dynamic_slice_in_dim(masked, column_start, HEAD, 2)
        key_block = jnp.concatenate(
            [
                lax.dynamic_slice_in_dim(key_pick, column_start, HEAD, 2),
                lax.dynamic_slice_in_dim(k_branch, column_start, HEAD, 2),
            ],
            1,
        )
        value_block = jnp.concatenate(
            [
                lax.dynamic_slice_in_dim(value_pick, column_start, HEAD, 2),
                lax.dynamic_slice_in_dim(v_branch, column_start, HEAD, 2),
            ],
            1,
        )
        scores = (
            jnp.einsum("sie,sje->sij", query_head, key_block, preferred_element_type=jnp.float32)
            * score_scale
        )
        scores = jnp.where(allowed, scores, -jnp.inf)
        row_max = jnp.max(scores, -1, keepdims=True)
        log_total = row_max + jnp.log(jnp.sum(jnp.exp(scores - row_max), -1, keepdims=True))
        exact_probs = jnp.exp(scores - log_total)
        weights = exact_probs.astype(jnp.bfloat16)
        attended = jnp.einsum(
            "sij,sje->sie", weights, value_block, preferred_element_type=jnp.float32
        )
        row_delta = jnp.sum(cotangent_head.astype(jnp.float32) * attended, -1, keepdims=True)
        grad_prob = jnp.einsum(
            "sie,sje->sij", cotangent_head, value_block, preferred_element_type=jnp.float32
        )
        grad_score = (exact_probs * (grad_prob - row_delta)).astype(jnp.bfloat16)
        grad_q = (
            jnp.einsum("sij,sje->sie", grad_score, key_block, preferred_element_type=jnp.float32)
            * score_scale
        ).astype(jnp.bfloat16)
        grad_k = (
            jnp.einsum("sij,sie->sje", grad_score, query_head, preferred_element_type=jnp.float32)
            * score_scale
        )
        grad_v = jnp.einsum(
            "sij,sie->sje", weights, cotangent_head, preferred_element_type=jnp.float32
        )
        branch_k = grad_k[:, prefix_rows:].astype(jnp.bfloat16)
        branch_v = grad_v[:, prefix_rows:].astype(jnp.bfloat16)
        return (
            grad_q,
            branch_k,
            branch_v,
            by_prefix(grad_k[:, :prefix_rows]),
            by_prefix(grad_v[:, :prefix_rows]),
        )

    head_results = lax.map(per_head, jnp.arange(local_heads, dtype=jnp.int32))
    query_grad = merge_heads(head_results[0])
    branch_key_grad = merge_heads(head_results[1])
    branch_value_grad = merge_heads(head_results[2])
    summed_k, summed_v = (
        lax.psum_scatter(merge_prefix(head_results[3]), "seq", scatter_dimension=0, tiled=True),
        lax.psum_scatter(merge_prefix(head_results[4]), "seq", scatter_dimension=0, tiled=True),
    )
    return (
        query_grad,
        branch_key_grad,
        branch_value_grad,
        summed_k.astype(jnp.bfloat16),
        summed_v.astype(jnp.bfloat16),
    )


def solution(mesh):
    in_specs = (
        P("seq", None, "mp"),
        P("seq", None, "mp"),
        P("seq", None, "mp"),
        P("seq", "mp", None),
        P("seq", None, "mp"),
        P("seq", None, "mp"),
        P(),
        P(),
    )
    out_specs = (
        P("seq", None, "mp"),
        P("seq", None, "mp"),
        P("seq", None, "mp"),
        P("seq", None, "mp"),
        P("seq", None, "mp"),
    )
    return jax.shard_map(body, mesh=mesh, in_specs=in_specs, out_specs=out_specs, check_vma=False)
```

profile of v0, /device:TPU:0, one launch (start us, length us, event | category | flops | bytes accessed | tf_op | source)
XLA Modules:
  0.0 265.0 jit_solution(14728028423991876309)
XLA Ops:
  7.2 2.2 copy.38
  9.4 1.7 reshape.142
  11.1 4.2 %all-to-all-start = ((bf16[4,2,16384]{2,1,0:T(2,128)(2,1)}), bf16[4,2,16384]{2,1,0:T(2,128)(2,1)S(1)}, u32[]{:S(2)}, u32[]{:S(2)}) async-start(bf16[4,2,16384]{2,1,0:T(2,128)(2,1)} %reshape.142), calls=%async_computation | async-start | bytes 524288 | tf_op jit(solution)/shard_map/all_to_all | solution.py:46
  15.4 33.2 %all_gather.6 = bf16[768,1,512]{2,0,1:T(8,128)(2,1)S(1)} all-gather(bf16[96,1,512]{2,0,1:T(8,128)(2,1)S(1)} %copy-done.5), channel_id=1, replica_groups=mesh['seq'=8,'mp'=4] {'seq'}, dimensions={0}, use_global_device_ids=true | all-gather | bytes 884736 | tf_op jit(solution)/shard_map/all_gather | solution.py:50
  48.8 32.0 %all_gather.7 = bf16[768,1,512]{2,0,1:T(8,128)(2,1)S(1)} all-gather(bf16[96,1,512]{2,0,1:T(8,128)(2,1)S(1)} %copy-done.6), channel_id=1, replica_groups=mesh['seq'=8,'mp'=4] {'seq'}, dimensions={0}, use_global_device_ids=true | all-gather | bytes 884736 | tf_op jit(solution)/shard_map/all_gather | solution.py:51
  81.3 1.5 reshape.143
  82.8 3.4 %copy.39 = bf16[2,4,32,512]{3,2,1,0:T(8,128)(2,1)} copy(bf16[2,4,32,512]{2,0,3,1:T(2,128)(2,1)} %bitcast.78) | data formatting | bytes 524288 | tf_op jit(solution)/shard_map/all_to_all | solution.py:46
  86.2 1.1 bitcast_select_fusion
  87.3 32.1 %while.19 = (s32[]{:T(128)}, bf16[4,2,128,128]{3,2,1,0:T(8,128)(2,1)}, bf16[4,2,128,128]{3,2,1,0:T(8,128)(2,1)}, bf16[4,2,128,128]{3,2,1,0:T(8,128)(2,1)}, f32[4...) while((s32[]{:T(128)}, ...), condition=%wide.region_5.6_spmd.clone, body=%wide.region_1.5_spmd.clone.sunk | while | flops 359677440 | bytes 15776563 | solution.py:116
  88.6 0.9 constant_dynamic-slice_fusion.10
  89.5 0.8 constant_dynamic-slice_fusion.8
  92.0 0.9 fusion.69
  94.3 1.0 fusion.72
  96.6 0.9 constant_dynamic-slice_fusion.10
  100.0 0.9 fusion.69
  102.3 1.0 fusion.72
  104.6 0.9 constant_dynamic-slice_fusion.10
  105.5 0.8 constant_dynamic-slice_fusion.8
  108.0 0.9 fusion.69
  110.4 1.0 fusion.72
  112.6 0.9 constant_dynamic-slice_fusion.10
  116.0 0.9 fusion.69
  118.4 1.0 fusion.72
  119.4 2.8 %copy_bitcast_fusion = f32[768,1,512]{2,0,1:T(8,128)} fusion(f32[4,768,1,128]{3,1,2,0:T(8,128)} %get-tuple-element.85), kind=kLoop, calls=%fused_computation.50 | loop fusion | bytes 3145728 | tf_op jit(solution)/shard_map/reshape | solution.py:29
  122.2 1.3 copy-done
  123.5 1.4 copy_bitcast_fusion.1
  124.9 0.9 copy-done.2
  126.6 0.8 copy_bitcast_fusion.2
  127.4 61.5 %reduce-scatter.5.cloned.1.call-done = f32[96,1,512]{2,0,1:T(8,128)} async-done(((f32[768,1,512]{2,0,1:T(8,128)}), f32[96,1,512]{2,0,1:T(8,128)}) %reduce-scatter.5.cloned.1.call-update) | async-done | bytes 196624 | tf_op jit(solution)/shard_map/reduce_scatter | solution.py:122
  189.0 1.6 convert_element_type.21
  190.6 66.0 %reduce-scatter.3.cloned.1.call-done = f32[96,1,512]{2,0,1:T(8,128)} async-done(((f32[768,1,512]{2,0,1:T(8,128)}), f32[96,1,512]{2,0,1:T(8,128)}) %reduce-scatter.3.cloned.1.call-update) | async-done | bytes 196624 | tf_op jit(solution)/shard_map/reduce_scatter | solution.py:121
  256.6 1.6 convert_element_type.20
  (90 shorter events, 17.8 us)
Async XLA Ops:
  7.2 8.2 %copy-start.5 = (bf16[96,1,512]{2,0,1:T(8,128)(2,1)S(1)}, bf16[96,1,512]{2,0,1:T(8,128)(2,1)}, u32[]{:S(2)}) copy-start(bf16[96,1,512]{2,0,1:T(8,128)(2,1)} %param.14) | copy-start | bytes 294916
  11.1 70.2 %all-to-all-start = ((bf16[4,2,16384]{2,1,0:T(2,128)(2,1)}), bf16[4,2,16384]{2,1,0:T(2,128)(2,1)S(1)}, u32[]{:S(2)}, u32[]{:S(2)}) async-start(bf16[4,2,16384]{2,1,0:T(2,128)(2,1)} %reshape.142), calls=%async_computation | async-start | bytes 524288 | tf_op jit(solution)/shard_map/all_to_all | solution.py:46
  15.3 173.7 %reduce-scatter.5.cloned.1.call-start = ((), (), s32[]{:S(2)}) async-start(), calls=%async_computation.4 | async-start | bytes 1769472 | tf_op jit(solution)/shard_map/reduce_scatter | solution.py:122
  15.4 33.4 %copy-start.6 = (bf16[96,1,512]{2,0,1:T(8,128)(2,1)S(1)}, bf16[96,1,512]{2,0,1:T(8,128)(2,1)}, u32[]{:S(2)}) copy-start(bf16[96,1,512]{2,0,1:T(8,128)(2,1)} %param.15) | copy-start | bytes 294916
  48.8 32.2 %copy-start.7 = (s32[16]{0:T(128)S(1)}, s32[16]{0:T(128)}, u32[]{:S(2)}) copy-start(s32[16]{0:T(128)} %param.16) | copy-start | bytes 196
  48.8 32.3 %copy-start.8 = (s32[16]{0:T(128)S(1)}, s32[16]{0:T(128)}, u32[]{:S(2)}) copy-start(s32[16]{0:T(128)} %param.17) | copy-start | bytes 196
  88.5 2.0 copy-start.1
  96.5 2.0 copy-start.1
  104.6 2.0 copy-start.1
  112.6 2.0 copy-start.1
  122.1 1.4 copy-start
  122.1 134.4 %reduce-scatter.3.cloned.1.call-start = ((), (), s32[]{:S(2)}) async-start(), calls=%async_computation.3 | async-start | bytes 1769472 | tf_op jit(solution)/shard_map/reduce_scatter | solution.py:121
  124.9 0.9 copy-start.2
  124.9 1.7 copy-start.3
  124.9 1.7 copy-start.4
Sparse Core Ops, SparseCore 0:
  122.3 66.6 reduce-scatter.4
  192.8 63.7 reduce-scatter.2
where the time goes:
time: 266 us; the launch traced here: 265 us
  waiting for transfers between devices  128 us (48%)
  blocking collectives  65.2 us (25%)
  local copies, waits for them, and re-layouts  29.4 us (11%)
  between operations  14.2 us (5%)
  matrix products  11.3 us (4%)
  other arithmetic  10.1 us (4%)
  starting transfers between devices  4.25 us (2%)
  loops' own time  2.9 us (1%)
    reduce_scatter x1, waiting for transfers between devices, body(): lax.psum_scatter(merge_prefix(head_results[3]), 'seq', scatter_dimension=...  66 us
    reduce_scatter x1, waiting for transfers between devices, body(): lax.psum_scatter(merge_prefix(head_results[4]), 'seq', scatter_dimension=...  61.5 us
    all_gather x1, blocking collectives, body(): lax.all_gather(k_prefix, 'seq', axis=0, tiled=True)  33.2 us
    all_gather x1, blocking collectives, body(): lax.all_gather(v_prefix, 'seq', axis=0, tiled=True)  32 us
    unnamed x19, local copies, waits for them, and re-layouts  7.68 us
  transfers between devices with their start and end apart: 3, of which 2 were waited for; matrix products, arithmetic and copies ran while one was open for 2% of the time, Pallas kernels for 0%

commit v1 on v0

--- a/solution.py
+++ b/solution.py
@@ -1,11 +1,519 @@
+import functools
 import math
 
 import jax
 import jax.numpy as jnp
 from jax import lax
+from jax.experimental import pallas as pl
+from jax.experimental.pallas import tpu as pltpu
 from jax.sharding import PartitionSpec as P
 
 HEAD = 128
+MESH = pl.DeviceIdType.MESH
+F32 = jnp.float32
+BF16 = jnp.bfloat16
+VMEM_LIMIT = 56 * 1024 * 1024
+
+
+def dot_nt(a, b):
+    return lax.dot_general(a, b, (((1,), (1,)), ((), ())), preferred_element_type=F32)
+
+
+def dot_nn(a, b):
+    return lax.dot_general(a, b, (((1,), (0,)), ((), ())), preferred_element_type=F32)
+
+
+def dot_tn(a, b):
+    return lax.dot_general(a, b, (((0,), (0,)), ((), ())), preferred_element_type=F32)
+
+
+def fused_kernel(
+    nseq,
+    nmp,
+    slots_ref,
+    lens_ref,
+    q_in,
+    k_in,
+    v_in,
+    do_ref,
+    kp_ref,
+    vp_ref,
+    dq_out,
+    dbk_out,
+    dbv_out,
+    dpk_ref,
+    dpv_ref,
+    kv,
+    dob,
+    dom,
+    st,
+    dp,
+    sb,
+    db,
+    mx,
+    wt,
+    ds,
+    wb,
+    dsb,
+    part,
+    ysend,
+    yrecv,
+    zsend,
+    zrecv,
+    q_ref,
+    k_ref,
+    v_ref,
+    dq_ref,
+    dbk_ref,
+    dbv_ref,
+    a_send,
+    a_recv,
+    d_send,
+    d_recv,
+    y_send,
+    y_recv,
+    z_send,
+    z_recv,
+    own_sem,
+):
+    slots, frames, cols = q_in.shape
+    heads = cols // HEAD
+    queries = slots * frames
+    rows = kp_ref.shape[0]
+    nz = nseq // 2
+    scale = 1.0 / math.sqrt(HEAD)
+    me = lax.axis_index("seq")
+    m = lax.axis_index("mp")
+    z = me // 2
+    y = lax.rem(me, 2)
+    oy = 1 - y
+    up, down, across = me + 2, me - 2, z * 2 + oy
+    has_up = z < nz - 1
+    has_down = z > 0
+
+    def chunk(zz, yy):
+        return zz * 2 + yy
+
+    pairs = ((q_in, q_ref), (k_in, k_ref), (v_in, v_ref))
+    loads = [pltpu.make_async_copy(a, b, own_sem.at[i]) for i, (a, b) in enumerate(pairs)]
+    pairs = ((dq_ref, dq_out), (dbk_ref, dbk_out), (dbv_ref, dbv_out))
+    stores = [pltpu.make_async_copy(a, b, own_sem.at[3 + i]) for i, (a, b) in enumerate(pairs)]
+
+    barrier = pltpu.get_barrier_semaphore()
+
+    def greet(seq_index, mp_index):
+        pl.semaphore_signal(barrier, inc=1, device_id=(seq_index, mp_index), device_id_type=MESH)
+
+    for step in range(1, nmp):
+        greet(me, lax.rem(m + step, nmp))
+    greet(across, m)
+
+    @pl.when(has_up)
+    def _():
+        greet(up, m)
+
+    @pl.when(has_down)
+    def _():
+        greet(down, m)
+
+    for load in loads:
+        load.start()
+    kv[0, me] = kp_ref[...]
+    kv[1, me] = vp_ref[...]
+    peers = nmp + jnp.where(has_up, 1, 0) + jnp.where(has_down, 1, 0)
+    pl.semaphore_wait(barrier, peers)
+
+    def ag_copy(side, which, zz, yy, target):
+        c = chunk(zz, yy)
+        return pltpu.make_async_remote_copy(
+            src_ref=kv.at[which, c],
+            dst_ref=kv.at[which, c],
+            send_sem=a_send.at[side, which, zz],
+            recv_sem=a_recv.at[which, c],
+            device_id=(target, m),
+            device_id_type=MESH,
+        )
+
+    def do_copy(sender, target, src_block):
+        return pltpu.make_async_remote_copy(
+            src_ref=do_ref.at[:, :, pl.ds(pl.multiple_of(src_block * cols, 128), cols)],
+            dst_ref=dob.at[sender],
+            send_sem=d_send.at[target],
+            recv_sem=d_recv.at[sender],
+            device_id=(me, target),
+            device_id_type=MESH,
+        )
+
+    for which in range(2):
+
+        @pl.when(has_up)
+        def _():
+            ag_copy(0, which, z, y, up).start()
+
+        @pl.when(has_down)
+        def _():
+            ag_copy(1, which, z, y, down).start()
+
+        ag_copy(2, which, z, y, across).start()
+    for step in range(1, nmp):
+        target = lax.rem(m + step, nmp)
+        do_copy(m, target, target).start()
+    dob[m] = do_ref[:, :, pl.ds(pl.multiple_of(m * cols, 128), cols)]
+
+    def head_cols(h):
+        return slice(h * HEAD, (h + 1) * HEAD)
+
+    def q_head(h):
+        return q_ref[:, :, head_cols(h)].reshape(queries, HEAD)
+
+    def fold_max(x):
+        return jnp.max(x.reshape(x.shape[0] // 8, 8, x.shape[1]), axis=0)
+
+    def fold_sum(x):
+        return jnp.sum(x.reshape(x.shape[0] // 8, 8, x.shape[1]), axis=0)
+
+    for load in loads:
+        load.wait()
+    key_pos = lax.broadcasted_iota(jnp.int32, (frames, frames), 0)
+    query_pos = lax.broadcasted_iota(jnp.int32, (frames, frames), 1)
+    seen = key_pos <= query_pos
+    for h in range(heads):
+        for s in range(slots):
+            scores = dot_nt(k_ref[s, :, head_cols(h)], q_ref[s, :, head_cols(h)])
+            scores = jnp.where(seen, scores, -jnp.inf)
+            sb[h, :, s * frames : (s + 1) * frames] = scores
+            mx[h, :, s * frames : (s + 1) * frames] = fold_max(scores)
+
+    for step in range(1, nmp):
+        sender = lax.rem(m + nmp - step, nmp)
+        do_copy(sender, sender, m).wait_recv()
+    row_at = lax.broadcasted_iota(jnp.int32, (frames, cols), 0)
+    for s in range(slots):
+        length = lens_ref[slots_ref[me * slots + s]]
+        rows_in = dob[:, s].reshape(frames, cols)
+        dom[s * frames : (s + 1) * frames, :] = jnp.where(
+            row_at < length, rows_in, jnp.zeros_like(rows_in)
+        )
+    for h in range(heads):
+        for s in range(slots):
+            db[h, :, s * frames : (s + 1) * frames] = dot_nt(
+                v_ref[s, :, head_cols(h)], dom[s * frames : (s + 1) * frames, head_cols(h)]
+            )
+
+    def take_chunk(c):
+        for h in range(heads):
+            scores = dot_nt(kv[0, c, :, head_cols(h)], q_head(h))
+            st[h, c] = scores
+            mx[h] = jnp.maximum(mx[h], fold_max(scores))
+            dp[h, c] = dot_nt(kv[1, c, :, head_cols(h)], dom[:, head_cols(h)])
+
+    def wait_z(zz):
+        for which in range(2):
+            ag_copy(2, which, zz, y, across).wait_recv()
+
+    def take_across(zz):
+        for which in range(2):
+            ag_copy(2, which, zz, oy, across).wait_recv()
+        take_chunk(chunk(zz, oy))
+
+    take_chunk(me)
+    for t in range(1, nz):
+        below, above = z - t, z + t
+
+        @pl.when(below >= 0)
+        def _():
+            for which in range(2):
+                ag_copy(0, which, below, y, across).wait_recv()
+
+                @pl.when(has_up)
+                def _():
+                    ag_copy(0, which, below, y, up).start()
+
+                ag_copy(2, which, below, y, across).start()
+
+        @pl.when(above < nz)
+        def _():
+            for which in range(2):
+                ag_copy(1, which, above, y, across).wait_recv()
+
+                @pl.when(has_down)
+                def _():
+                    ag_copy(1, which, above, y, down).start()
+
+                ag_copy(2, which, above, y, across).start()
+
+        @pl.when(below >= 0)
+        def _():
+            take_chunk(chunk(below, y))
+
+        @pl.when(above < nz)
+        def _():
+            take_chunk(chunk(above, y))
+
+        if t == 1:
+            take_across(z)
+        else:
+
+            @pl.when(z - (t - 1) >= 0)
+            def _():
+                take_across(z - (t - 1))
+
+            @pl.when(z + (t - 1) < nz)
+            def _():
+                take_across(z + (t - 1))
+
+    @pl.when(z - (nz - 1) >= 0)
+    def _():
+        take_across(z - (nz - 1))
+
+    @pl.when(z + (nz - 1) < nz)
+    def _():
+        take_across(z + (nz - 1))
+
+    for h in range(heads):
+        top = jnp.max(mx[h], axis=0, keepdims=True)
+        total = jnp.zeros((8, queries), F32)
+        delta = jnp.zeros((8, queries), F32)
+        for c in range(nseq):
+            e = jnp.exp((st[h, c] - top) * scale)
+            st[h, c] = e
+            total = total + fold_sum(e)
+            delta = delta + fold_sum(e * dp[h, c])
+        e = jnp.exp((sb[h] - top) * scale)
+        sb[h] = e
+        total = total + fold_sum(e)
+        delta = delta + fold_sum(e * db[h])
+        inverse = 1.0 / jnp.sum(total, axis=0, keepdims=True)
+        delta = jnp.sum(delta, axis=0, keepdims=True) * inverse
+        for c in range(nseq):
+            p = st[h, c] * inverse
+            wt[h, c] = p.astype(BF16)
+            ds[h, c] = (p * (dp[h, c] - delta)).astype(BF16)
+        p = sb[h] * inverse
+        wb[h] = p.astype(BF16)
+        dsb[h] = (p * (db[h] - delta)).astype(BF16)
+
+    def y_copy(which, zz):
+        return pltpu.make_async_remote_copy(
+            src_ref=ysend.at[which, zz],
+            dst_ref=yrecv.at[which, zz],
+            send_sem=y_send.at[which, zz],
+            recv_sem=y_recv.at[which, zz],
+            device_id=(across, m),
+            device_id_type=MESH,
+        )
+
+    order = []
+    low, high = 0, nz - 1
+    for _ in range(nz):
+        take_high = high - z >= z - low
+        order.append(jnp.where(take_high, high, low))
+        low, high = jnp.where(take_high, low, low + 1), jnp.where(take_high, high - 1, high)
+    for zz in order:
+        c = chunk(zz, oy)
+        for h in range(heads):
+            ysend[0, zz, :, head_cols(h)] = (dot_nn(ds[h, c], q_head(h)) * scale).astype(BF16)
+        y_copy(0, zz).start()
+        for h in range(heads):
+            ysend[1, zz, :, head_cols(h)] = dot_nn(wt[h, c], dom[:, head_cols(h)]).astype(BF16)
+        y_copy(1, zz).start()
+    for zz in order:
+        c = chunk(zz, y)
+        for h in range(heads):
+            part[0, zz, :, head_cols(h)] = dot_nn(ds[h, c], q_head(h)) * scale
+            part[1, zz, :, head_cols(h)] = dot_nn(wt[h, c], dom[:, head_cols(h)])
+
+    def z_copy(side, which, zz, target):
+        return pltpu.make_async_remote_copy(
+            src_ref=zsend.at[side, which, zz],
+            dst_ref=zrecv.at[side, which, zz],
+            send_sem=z_send.at[side, which, zz],
+            recv_sem=z_recv.at[side, which, zz],
+            device_id=(target, m),
+            device_id_type=MESH,
+        )
+
+    def relay(side, zz, has_source, target):
+        for which in range(2):
+            y_copy(which, zz).wait_recv()
+            part[which, zz] = part[which, zz] + yrecv[which, zz].astype(F32)
+
+            @pl.when(has_source)
+            def _():
+                z_copy(side, which, zz, target).wait_recv()
+                part[which, zz] = part[which, zz] + zrecv[side, which, zz].astype(F32)
+
+            zsend[side, which, zz] = part[which, zz].astype(BF16)
+            z_copy(side, which, zz, target).start()
+
+    def query_grads(h):
+        keys = kv[0, :, :, head_cols(h)].reshape(nseq * rows, HEAD)
+        grad = dot_tn(ds[h].reshape(nseq * rows, queries), keys)
+        for s in range(slots):
+            at = slice(s * frames, (s + 1) * frames)
+            own = dot_tn(dsb[h, :, at], k_ref[s, :, head_cols(h)])
+            dq_ref[s, :, head_cols(h)] = ((grad[at] + own) * scale).astype(BF16)
+            dbk_ref[s, :, head_cols(h)] = (
+                dot_nn(dsb[h, :, at], q_ref[s, :, head_cols(h)]) * scale
+            ).astype(BF16)
+            dbv_ref[s, :, head_cols(h)] = dot_nn(wb[h, :, at], dom[at, head_cols(h)]).astype(BF16)
+
+    for h in range(heads):
+        query_grads(h)
+    for store in stores:
+        store.start()
+    for zz in order[:-1]:
+
+        @pl.when(zz > z)
+        def _():
+            relay(0, zz, has_down, up)
+
+        @pl.when(zz < z)
+        def _():
+            relay(1, zz, has_up, down)
+
+    for which, out in ((0, dpk_ref), (1, dpv_ref)):
+        y_copy(which, z).wait_recv()
+        part[which, z] = part[which, z] + yrecv[which, z].astype(F32)
+
+        @pl.when(has_down)
+        def _():
+            z_copy(0, which, z, across).wait_recv()
+            part[which, z] = part[which, z] + zrecv[0, which, z].astype(F32)
+
+        @pl.when(has_up)
+        def _():
+            z_copy(1, which, z, across).wait_recv()
+            part[which, z] = part[which, z] + zrecv[1, which, z].astype(F32)
+
+        out[...] = part[which, z].astype(BF16)
+
+    for store in stores:
+        store.wait()
+    for step in range(1, nmp):
+        target = lax.rem(m + step, nmp)
+        do_copy(m, target, target).wait_send()
+    for zz in range(nz):
+        for which in range(2):
+            ag_copy(2, which, zz, y, across).wait_send()
+            y_copy(which, zz).wait_send()
+
+            @pl.when(jnp.logical_and(has_up, zz <= z))
+            def _():
+                ag_copy(0, which, zz, y, up).wait_send()
+
+            @pl.when(jnp.logical_and(has_down, zz >= z))
+            def _():
+                ag_copy(1, which, zz, y, down).wait_send()
+
+            @pl.when(z < zz)
+            def _():
+                z_copy(0, which, zz, up).wait_send()
+
+            @pl.when(z > zz)
+            def _():
+                z_copy(1, which, zz, down).wait_send()
+
+
+def hand_over(*refs):
+    count = len(refs) // 2
+    sems = refs[-1]
+    copies = [
+        pltpu.make_async_copy(refs[i], refs[count + i], sems.at[i]) for i in range(count)
+    ]
+    for copy in copies:
+        copy.start()
+    for copy in copies:
+        copy.wait()
+
+
+def scratch_list(nseq, nmp, slots, frames, cols, rows):
+    heads, queries, nz = cols // HEAD, slots * frames, nseq // 2
+    return [
+        ((2, nseq, rows, cols), BF16),
+        ((nmp, slots, frames // nmp, cols), BF16),
+        ((queries, cols), BF16),
+        ((heads, nseq, rows, queries), F32),
+        ((heads, nseq, rows, queries), F32),
+        ((heads, frames, queries), F32),
+        ((heads, frames, queries), F32),
+        ((heads, 8, queries), F32),
+        ((heads, nseq, rows, queries), BF16),
+        ((heads, nseq, rows, queries), BF16),
+        ((heads, frames, queries), BF16),
+        ((heads, frames, queries), BF16),
+        ((2, nz, rows, cols), F32),
+        ((2, nz, rows, cols), BF16),
+        ((2, nz, rows, cols), BF16),
+        ((2, 2, nz, rows, cols), BF16),
+        ((2, 2, nz, rows, cols), BF16),
+    ] + [((slots, frames, cols), BF16)] * 6
+
+
+def fused_body(nseq, nmp, q_branch, k_branch, v_branch, d_out, k_prefix, v_prefix, slot_branch, branch_len):
+    slots, frames, cols = q_branch.shape
+    rows = k_prefix.shape[0]
+    nz = nseq // 2
+    scratch = [
+        pltpu.VMEM(shape, dtype)
+        for shape, dtype in scratch_list(nseq, nmp, slots, frames, cols, rows)
+    ]
+    dma = pltpu.SemaphoreType.DMA
+    sems = [
+        dma((3, 2, nz)),
+        dma((2, nseq)),
+        dma((nmp,)),
+        dma((nmp,)),
+        dma((2, nz)),
+        dma((2, nz)),
+        dma((2, 2, nz)),
+        dma((2, 2, nz)),
+        dma((6,)),
+    ]
+    vmem = pl.BlockSpec(memory_space=pltpu.VMEM)
+    smem = pl.BlockSpec(memory_space=pltpu.SMEM)
+    anywhere = pl.BlockSpec(memory_space=pl.ANY)
+    branch = jax.ShapeDtypeStruct((slots, frames, cols), BF16)
+    prefix = jax.ShapeDtypeStruct((rows, cols), BF16)
+    dq, dbk, dbv, dpk, dpv = pl.pallas_call(
+        functools.partial(fused_kernel, nseq, nmp),
+        out_shape=(branch, branch, branch, prefix, prefix),
+        in_specs=[smem] * 2 + [anywhere] * 3 + [vmem] * 3,
+        out_specs=(anywhere,) * 3 + (vmem,) * 2,
+        scratch_shapes=scratch + sems,
+        compiler_params=pltpu.CompilerParams(
+            collective_id=0, has_side_effects=True, vmem_limit_bytes=VMEM_LIMIT
+        ),
+        name="attention_backward",
+    )(
+        slot_branch,
+        branch_len,
+        q_branch,
+        k_branch,
+        v_branch,
+        d_out,
+        k_prefix[:, 0],
+        v_prefix[:, 0],
+    )
+    dq, dbk, dbv, dpk, dpv = pl.pallas_call(
+        hand_over,
+        out_shape=(branch, branch, branch, prefix, prefix),
+        in_specs=[vmem] * 5,
+        out_specs=(anywhere,) * 5,
+        scratch_shapes=[dma((5,))],
+        name="hand_over",
+    )(dq, dbk, dbv, dpk, dpv)
+    return dq, dbk, dbv, dpk[:, None], dpv[:, None]
+
+
+def fits(nseq, nmp, slots, frames, cols, rows):
+    if nseq % 2 or rows % 16 or (frames // nmp) % 16 or cols % HEAD:
+        return False
+    held = sum(
+        math.prod(shape) * jnp.dtype(dtype).itemsize
+        for shape, dtype in scratch_list(nseq, nmp, slots, frames, cols, rows)
+    )
+    return held < VMEM_LIMIT // 2
 
 
 def pick_prefix(gathered, slot_count):
@@ -31,7 +539,7 @@
     )
 
 
-def body(q_branch, k_branch, v_branch, d_out, k_prefix, v_prefix, slot_branch, branch_len):
+def plain_body(q_branch, k_branch, v_branch, d_out, k_prefix, v_prefix, slot_branch, branch_len):
     score_scale = 1.0 / math.sqrt(HEAD)
     slot_count = q_branch.shape[0]
     frames = q_branch.shape[1]
@@ -130,6 +638,13 @@
     )
 
 
+def body(nseq, nmp, *arrays):
+    slots, frames, cols = arrays[0].shape
+    if fits(nseq, nmp, slots, frames, cols, arrays[4].shape[0]):
+        return fused_body(nseq, nmp, *arrays)
+    return plain_body(*arrays)
+
+
 def solution(mesh):
     in_specs = (
         P("seq", None, "mp"),
@@ -148,4 +663,10 @@
         P("seq", None, "mp"),
         P("seq", None, "mp"),
     )
-    return jax.shard_map(body, mesh=mesh, in_specs=in_specs, out_specs=out_specs, check_vma=False)
+    return jax.shard_map(
+        functools.partial(body, mesh.shape["seq"], mesh.shape["mp"]),
+        mesh=mesh,
+        in_specs=in_specs,
+        out_specs=out_specs,
+        check_vma=False,
+    )

time: 266 us -> 51 us (0.19)
  waiting for transfers between devices: 128 us -> 0 us
  blocking collectives: 65.2 us -> 0 us
  Pallas kernels: 0 us -> 50.2 us
  local copies, waits for them, and re-layouts: 29.4 us -> 0 us
  between operations: 14.2 us -> 0.64 us
  matrix products: 11.3 us -> 0 us
  other arithmetic: 10.1 us -> 0 us
  starting transfers between devices: 4.25 us -> 0 us
  loops' own time: 2.9 us -> 0 us
    reduce_scatter x2 -> x0, waiting for transfers between devices: 128 us -> none  [the longest x1 66 us: body(): lax.psum_scatter(merge_prefix(head_results[3]), 'seq', scatter_dimension=...]
    all_gather x2 -> x0, blocking collectives: 65.2 us -> none  [the longest x1 33.2 us: body(): lax.all_gather(k_prefix, 'seq', axis=0, tiled=True)]
    pallas_call x0 -> x2, Pallas kernels: none -> 50.2 us  [the longest x1 48.1 us: fused_body(): pl.pallas_call(functools.partial(fused_kernel, nseq, nmp), out_shape=(bra...]
    dot_general x24 -> x0, matrix products: 11.3 us -> none  [the longest x4 3.64 us: per_head(): jnp.einsum('sij,sje->sie', grad_score, key_block, preferred_element_type=...]
    dynamic_slice x21 -> x0, local copies, waits for them, and re-layouts: 9.84 us -> none  [the longest x4 3.57 us: per_head(): lax.dynamic_slice_in_dim(v_branch, column_start, HEAD, 2)]
    unnamed x19 -> x0, local copies, waits for them, and re-layouts: 7.68 us -> none
    reshape x4 -> x0, local copies, waits for them, and re-layouts: 5.73 us -> none  [the longest x2 4.15 us: merge_prefix(): jnp.transpose(stacked, (1, 2, 0, 3))]
    all_to_all x1 -> x0, starting transfers between devices: 4.21 us -> none  [body(): lax.all_to_all(d_out, 'mp', split_axis=2, concat_axis=1, tiled=True)]
  transfers between devices with their start and end apart: 3 -> 0, of which waited for: 2 -> 0; matrix products, arithmetic and copies ran while one was open for 2% -> 0% of each run, Pallas kernels for 0% -> 0%
where the time goes in v1:
time: 51 us; the launch traced here: 50.9 us
  Pallas kernels  50.2 us (98%)
  between operations  0.64 us (1%)
    pallas_call x1, Pallas kernels, fused_body(): pl.pallas_call(functools.partial(fused_kernel, nseq, nmp), out_shape=(bra...  48.1 us
    pallas_call x1, Pallas kernels, fused_body(): pl.pallas_call(hand_over, out_shape=(branch, branch, branch, prefix, pref...  2.15 us

profile of v1, /device:TPU:0, one launch (start us, length us, event | category | flops | bytes accessed | tf_op | source)
XLA Modules:
  0.0 50.9 jit_solution(2742840136460721228)
XLA Ops:
  0.6 48.1 %attention_backward.1 = (bf16[2,128,512]{2,1,0:T(8,128)(2,1)}, bf16[2,128,512]{2,1,0:T(8,128)(2,1)}, bf16[2,128,512]{2,1,0:T(8,128)(2,1)}, bf16[96,512]{1,0:T(8,128)(2,1)}, bf16[96,512]{1,0:T(8,128)(2,1)}) custom-call(s32[16]{0:T(128)} %slots_ref.1, s32[16]{0:T(128)} %lens_ref.1, bf16[2,128,512]{2,1,0:T(8,128)(2,1)} %q_in.1, bf16[2,128,512]{2,1,0:T(8,128)(2,1)} %k_in.1, ...), custom_call_target="tpu_custom_call" | custom-call | tf_op jit(solution)/shard_map/attention_backward/pallas_call | solution.py:478
  48.7 2.2 %hand_over.1 = (bf16[2,128,512]{2,1,0:T(8,128)(2,1)}, bf16[2,128,512]{2,1,0:T(8,128)(2,1)}, bf16[2,128,512]{2,1,0:T(8,128)(2,1)}, bf16[96,512]{1,0:T(8,128)(2,1)}, bf16[96,512]{1,0:T(8,128)(2,1)}) custom-call(bf16[2,128,512]{2,1,0:T(8,128)(2,1)} %get-tuple-element.15.refs_0_, bf16[2,128,512]{2,1,0:T(8,128)(2,1)} %get-tuple-element.16.refs_1_, ...), custom_call_target="tpu_custom_call" | custom-call | tf_op jit(solution)/shard_map/hand_over/pallas_call | solution.py:498
